TPU v7x, 32 devices: a whole 2x2x4 slice. The times are simulated.
32 devices in a mesh: lat: 16 (over z, x, core), ma: 2 (over y).
Axes of the slice: x: 2, y: 2, z: 4, core: 2. Of those that a mesh axis runs over, the one named last changes fastest.
Arguments:
- grad_fourier: bfloat16 [4, 1024, 2, 384], P('ma', 'lat'), may hold values from -6 to 6
- legendre: bfloat16 [4, 1024, 640], P('ma', 'lat'), may hold values from -0.1875 to 0.1875
- spectra: bfloat16 [640, 4, 2, 384], P('lat', None, None, 'ma'), may hold values from -3 to 3
- filter_weight: float32 [640, 2, 384], P('lat'), may hold values from -6 to 6
Outputs:
- input_grad: float32 [640, 4, 2, 384], P('lat', 'ma')
- weight_grad: float32 [640, 2, 384], P('lat', None, 'ma')
All inputs are finite; a program needn't handle non-finite values.
Results may differ from a plain program's by a relative error of at most 0.0006.
Values may be sent and summed in bfloat16 or wider, within the bound.
A program may use at most 64 MiB of HBM per device.

v0:
```python
import jax
import jax.numpy as jnp
from jax import lax
from jax.sharding import PartitionSpec as P


def pair_sums(stored, grads):
    real_store = stored[:, :, 0, :]
    imag_store = stored[:, :, 1, :]
    real_grad = grads[:, :, 0, :]
    imag_grad = grads[:, :, 1, :]
    return jnp.stack(
        [
            jnp.sum(real_store * real_grad + imag_store * imag_grad, axis=1),
            jnp.sum(real_store * imag_grad - imag_store * real_grad, axis=1),
        ],
        axis=1,
    )


def body(grad_fourier, legendre, spectra, filter_weight):
    orders_dev = legendre.shape[0]
    first_order = lax.axis_index("ma") * orders_dev
    degree_ids = lax.broadcasted_iota(jnp.int32, legendre.shape, 2)
    order_ids = lax.broadcasted_iota(jnp.int32, legendre.shape, 0) + first_order
    table = jnp.where(degree_ids >= order_ids, legendre, jnp.zeros_like(legendre))
    partial_value = jnp.einsum(
        "mal,marc->lmrc", table, grad_fourier, preferred_element_type=jnp.float32
    )
    grads = lax.psum_scatter(partial_value, "lat", scatter_dimension=0, tiled=True)
    real_grad = grads[:, :, 0, :]
    imag_grad = grads[:, :, 1, :]
    real_weight = filter_weight[:, None, 0, :]
    imag_weight = filter_weight[:, None, 1, :]
    input_grad = jnp.stack(
        [
            real_weight * real_grad + imag_weight * imag_grad,
            real_weight * imag_grad - imag_weight * real_grad,
        ],
        axis=2,
    )
    local_store = lax.all_to_all(spectra, "ma", split_axis=1, concat_axis=3, tiled=True)
    partial_weight = pair_sums(local_store.astype(jnp.float32), grads)
    weight_grad = lax.psum_scatter(partial_weight, "ma", scatter_dimension=2, tiled=True)
    return (input_grad, weight_grad)


def solution(mesh):
    in_specs = (
        P("ma", "lat", None, None),
        P("ma", "lat", None),
        P("lat", None, None, "ma"),
        P("lat", None, None),
    )
    out_specs = (P("lat", "ma", None, None), P("lat", None, "ma"))
    return jax.shard_map(body, mesh=mesh, in_specs=in_specs, out_specs=out_specs, check_vma=False)
```

profile of v0, /device:TPU:0, one launch (start us, length us, event | category | flops | bytes accessed | tf_op | source)
XLA Modules:
  0.0 106.0 jit_solution(15035284839424399578)
XLA Ops:
  7.2 0.0 copy-start
  7.2 0.0 reduce-scatter.5.cloned.1.call-start
  7.2 0.9 copy-done
  8.1 0.0 copy-start.1
  8.1 3.6 %convolution_bitcast_fusion = f32[640,2,2,384]{3,0,2,1:T(8,128)} fusion(bf16[2,64,2,384]{3,2,1,0:T(2,128)(2,1)S(1)} %copy-done, bf16[2,64,640]{2,1,0:T(8,128)(2,1)} %param.5, s32[2]{0:T(128)S(1)} %iota_add_fusion), kind=kOutput, calls=%fused_computation | convolution fusion | flops 125992960 | bytes 4292616 | tf_op jit(solution)/shard_map/mal,marc->lmrc/dot_general | solution.py:27
  11.7 0.0 reduce-scatter.5.cloned.1.call-update
  11.7 0.0 copy-done.1
  11.7 0.8 copy.18
  12.5 4.2 %all-to-all-start = ((bf16[40,4,2,192]{3,2,0,1:T(2,128)(2,1)}), bf16[40,4,2,192]{3,2,0,1:T(2,128)(2,1)S(1)}, u32[]{:S(2)}, u32[]{:S(2)}) async-start(bf16[40,4,2,192]{3,2,0,1:T(2,128)(2,1)} %copy.18), calls=%async_computation.1 | async-start | bytes 327680 | tf_op jit(solution)/shard_map/all_to_all | solution.py:42
  16.8 0.0 reduce-scatter.7.cloned.1.call-start
  16.8 0.0 copy-done.2
  16.8 0.1 fusion.7
  16.9 4.7 %all-to-all-done = bf16[40,4,2,192]{3,2,0,1:T(2,128)(2,1)S(1)} async-done(((bf16[40,4,2,192]{3,2,0,1:T(2,128)(2,1)}), bf16[40,4,2,192]{3,2,0,1:T(2,128)(2,1)S(1)}, u32[]{:S(2)}, u32[]{:S(2)}) %all-to-all-start) | async-done | bytes 122912 | tf_op jit(solution)/shard_map/all_to_all | solution.py:42
  21.6 0.2 copy.33
  21.7 0.2 reshape.14
  22.0 63.0 %reduce-scatter.5.cloned.1.call-done = f32[40,2,2,384]{3,0,2,1:T(8,128)} async-done(((f32[640,2,2,384]{3,0,2,1:T(8,128)}), f32[40,2,2,384]{3,0,2,1:T(8,128)}) %reduce-scatter.5.cloned.1.call-update) | async-done | bytes 245776 | tf_op jit(solution)/shard_map/reduce_scatter | solution.py:30
  85.0 1.0 add_reduce_fusion
  86.1 0.2 copy.23
  86.3 0.9 reshape.17
  87.2 0.0 reduce-scatter.7.cloned.1.call-update
  87.3 0.8 copy.20
  88.1 9.3 %reduce-scatter.7.cloned.1.call-done = f32[192,80]{1,0:T(8,128)} async-done(((f32[384,80]{1,0:T(8,128)}), f32[192,80]{1,0:T(8,128)}) %reduce-scatter.7.cloned.1.call-update) | async-done | bytes 61456
  97.3 1.0 reshape.18
  98.4 0.8 copy.21
  (5 shorter events, 0.1 us)
Async XLA Ops:
  7.2 0.9 copy-start
  7.2 77.8 %reduce-scatter.5.cloned.1.call-start = ((), (), s32[]{:S(2)}) async-start(), calls=%async_computation.3 | async-start | bytes 4177920 | tf_op jit(solution)/shard_map/reduce_scatter | solution.py:30
  8.1 3.6 %copy-start.1 = (bf16[40,4,2,192]{3,2,1,0:T(2,128)(2,1)S(1)}, bf16[40,4,2,192]{3,2,1,0:T(2,128)(2,1)}, u32[]{:S(2)}) copy-start(bf16[40,4,2,192]{3,2,1,0:T(2,128)(2,1)} %param.6) | copy-start | bytes 368644
  8.1 8.7 %copy-start.2 = (f32[40,2,384]{2,1,0:T(2,128)S(1)}, f32[40,2,384]{2,1,0:T(2,128)}, u32[]{:S(2)}) copy-start(f32[40,2,384]{2,1,0:T(2,128)} %param.7) | copy-start | bytes 368644
  12.5 9.0 %all-to-all-start = ((bf16[40,4,2,192]{3,2,0,1:T(2,128)(2,1)}), bf16[40,4,2,192]{3,2,0,1:T(2,128)(2,1)S(1)}, u32[]{:S(2)}, u32[]{:S(2)}) async-start(bf16[40,4,2,192]{3,2,0,1:T(2,128)(2,1)} %copy.18), calls=%async_computation.1 | async-start | bytes 327680 | tf_op jit(solution)/shard_map/all_to_all | solution.py:42
  16.8 80.6 %reduce-scatter.7.cloned.1.call-start = ((), (), s32[]{:S(2)}) async-start(), calls=%async_computation.4 | async-start | bytes 294912
Sparse Core Ops, SparseCore 0:
  11.9 73.0 reduce-scatter.4
  87.3 9.9 reduce-scatter.6
where the time goes:
time: 106 us
  waiting for transfers between devices  77 us (73%)
  between operations  14.1 us (13%)
  local copies, waits for them, and re-layouts  5.9 us (6%)
  starting transfers between devices  4.27 us (4%)
  matrix products  3.61 us (3%)
  other arithmetic  1.08 us (1%)
    reduce_scatter x1, waiting for transfers between devices, body(): lax.psum_scatter(partial_value, 'lat', scatter_dimension=0, tiled=True)  63 us
    unnamed x3, waiting for transfers between devices  9.31 us
    unnamed x12, local copies, waits for them, and re-layouts  5.38 us
    all_to_all x1, waiting for transfers between devices, body(): lax.all_to_all(spectra, 'ma', split_axis=1, concat_axis=3, tiled=True)  4.68 us
    all_to_all x1, starting transfers between devices, body(): lax.all_to_all(spectra, 'ma', split_axis=1, concat_axis=3, tiled=True)  4.23 us
    dot_general x1, matrix products, body(): jnp.einsum('mal,marc->lmrc', table, grad_fourier, preferred_element_type=...  3.61 us
  transfers between devices with their start and end apart: 3, of which 3 were waited for; matrix products, arithmetic and copies ran while one was open for 2% of the time, Pallas kernels for 0%

commit v1 on v0

v1 whole, which is shorter than its diff:
```python
import functools

import jax
import jax.numpy as jnp
from jax import lax
from jax.experimental import pallas as pl
from jax.experimental.pallas import tpu as pltpu
from jax.sharding import PartitionSpec as P

MESH = pl.DeviceIdType.MESH
GROUP = 8
CORE, NEAR, FAR = 1, 2, 4


def kernel(sizes, leg_ref, rows_ref, spec_ref, grads_ref, wgrad_ref, tab_send, tab_all, lhs, rows_all, part, part_recv,
           spec_all, wpart, wrecv, tab_ssem, tab_rsem, row_ssem, row_rsem, part_ssem, part_rsem, spec_ssem, spec_rsem,
           w_ssem, w_rsem):
    n, ma, orders, rows, deg, dq, chans = sizes
    blocks = n // GROUP
    chunks = 2 * orders
    width = chans // ma
    lat = lax.axis_index("lat")
    mine = lax.axis_index("ma")
    spot = lax.rem(lat, GROUP)
    block = lax.div(lat, GROUP)
    bits = [lax.rem(lax.div(spot, 1 << b), 2) for b in range(3)]

    def member(slot):
        at = 0
        for b in range(3):
            bit = 1 - bits[b] if slot >> b & 1 else bits[b]
            at = at + bit * (1 << b)
        return at

    def peer(slot):
        return (block * GROUP + member(slot), mine)

    def other_block(step):
        return lax.rem(block + step, blocks)

    def other_ma(step):
        return lax.rem(mine + step, ma)

    barrier = pltpu.get_barrier_semaphore()
    partners = [peer(slot) for slot in range(1, GROUP)]
    partners += [(other_block(step) * GROUP + spot, mine) for step in range(1, blocks)]
    partners += [(lat, other_ma(step)) for step in range(1, ma)]
    for device in partners:
        pl.semaphore_signal(barrier, inc=1, device_id=device, device_id_type=MESH)

    total = leg_ref.shape[2]
    degree = lax.broadcasted_iota(jnp.int32, (orders, rows, total), 2)
    order = lax.broadcasted_iota(jnp.int32, (orders, rows, total), 0) + mine * orders
    table = jnp.where(degree >= order, leg_ref[...].astype(jnp.float32), 0.0)
    turned = table.reshape(orders * rows, total).T
    for at in range(GROUP):
        parts = []
        for b in range(blocks):
            start = (b * GROUP + at) * deg
            part_rows = turned[start:start + deg]
            if dq > deg:
                part_rows = jnp.concatenate([part_rows, jnp.zeros((dq - deg, orders * rows), jnp.float32)], axis=0)
            parts.append(part_rows)
        tab_send[at] = jnp.concatenate(parts, axis=0).astype(jnp.bfloat16)
    pl.semaphore_wait(barrier, len(partners))

    def copy(src, dst, ssem, rsem, device):
        return pltpu.make_async_remote_copy(
            src_ref=src, dst_ref=dst, send_sem=ssem, recv_sem=rsem, device_id=device, device_id_type=MESH)

    tab_copies = {}
    for slot in (FAR, NEAR, FAR + NEAR, FAR + CORE, NEAR + CORE, FAR + NEAR + CORE, CORE):
        tab_copies[slot] = copy(tab_send.at[member(slot)], tab_all.at[slot], tab_ssem.at[slot], tab_rsem.at[slot], peer(slot))
        tab_copies[slot].start()

    row_copies = {}

    def send_rows(k, have, via):
        src = rows_ref.at[k] if have == 0 else rows_all.at[k, have]
        slot = have + via
        row_copies[k, slot] = copy(src, rows_all.at[k, slot], row_ssem.at[k, slot], row_rsem.at[k, slot], peer(via))
        row_copies[k, slot].start()

    def first(k):
        for via in (FAR, NEAR, CORE):
            send_rows(k, 0, via)

    first(0)
    first(1)
    spec_copies = []
    for step in range(1, ma):
        to = other_ma(step)
        spec_copies.append(copy(spec_ref.at[to], spec_all.at[mine], spec_ssem.at[step], spec_rsem.at[step], (lat, to)))
        spec_copies[-1].start()
    for k in range(2, chunks):
        first(k)
    spec_all[mine] = spec_ref[mine]
    for k in range(chunks):
        rows_all[k, 0] = rows_ref[k]

    def spread(k):
        row_copies[k, FAR].wait_recv()
        send_rows(k, FAR, NEAR)
        send_rows(k, FAR, CORE)
        row_copies[k, NEAR].wait_recv()
        send_rows(k, NEAR, CORE)

    def spread_last(k):
        row_copies[k, FAR + NEAR].wait_recv()
        send_rows(k, FAR + NEAR, CORE)

    part_copies = {}

    def multiply(k):
        m = k // 2
        if k == 0:
            for slot in tab_copies:
                tab_copies[slot].wait_recv()
            tabs = [tab_send[spot]] + [tab_all[slot] for slot in range(1, GROUP)]
            for order_at in range(orders):
                lhs[order_at] = jnp.concatenate(
                    [t.astype(jnp.float32)[:, order_at * rows:(order_at + 1) * rows] for t in tabs], axis=1
                ).astype(jnp.bfloat16)
        for slot in (CORE, NEAR + CORE, FAR + CORE, FAR + NEAR + CORE):
            row_copies[k, slot].wait_recv()
        product = jnp.dot(lhs[m], rows_all[k].reshape(GROUP * rows, chans), preferred_element_type=jnp.float32)
        part[k] = product.reshape(blocks, dq, chans)
        for step in range(1, blocks):
            to = other_block(step)
            part_copies[k, step] = copy(part.at[k, to], part_recv.at[k, step], part_ssem.at[k, step], part_rsem.at[k, step],
                                        (to * GROUP + spot, mine))
            part_copies[k, step].start()

    def finish(k):
        value = part[k, block]
        for step in range(1, blocks):
            part_copies[k, step].wait_recv()
            value = value + part_recv[k, step]
        grads_ref[k // 2, k % 2] = value

    def pair(m):
        if m == 0:
            for each in spec_copies:
                each.wait_recv()
        for q in range(ma):
            cut = slice(q * width, (q + 1) * width)
            real_grad = grads_ref[m, 0][:, cut]
            imag_grad = grads_ref[m, 1][:, cut]
            stored = spec_all[q].astype(jnp.float32)
            real_store = stored[2 * m * dq:(2 * m + 1) * dq]
            imag_store = stored[(2 * m + 1) * dq:(2 * m + 2) * dq]
            real = real_store * real_grad + imag_store * imag_grad
            imag = real_store * imag_grad - imag_store * real_grad
            if m == 0:
                wpart[q, 0] = real
                wpart[q, 1] = imag
            else:
                wpart[q, 0] += real
                wpart[q, 1] += imag

    def settle(k):
        finish(k)
        if k % 2:
            pair(k // 2)

    spread(0)
    spread_last(0)
    for k in range(chunks):
        if k + 1 < chunks:
            spread(k + 1)
        multiply(k)
        if k + 1 < chunks:
            spread_last(k + 1)
        if k >= 1:
            settle(k - 1)
    settle(chunks - 1)

    w_copies = []
    for step in range(1, ma):
        to = other_ma(step)
        w_copies.append(copy(wpart.at[to], wrecv.at[step], w_ssem.at[step], w_rsem.at[step], (lat, to)))
        w_copies[-1].start()
    weight = wpart[mine]
    for step in range(1, ma):
        w_copies[step - 1].wait_recv()
        weight = weight + wrecv[step]
    wgrad_ref[...] = weight

    for each in [*tab_copies.values(), *row_copies.values(), *part_copies.values(), *spec_copies, *w_copies]:
        each.wait_send()


def body(n, ma, grad_fourier, legendre, spectra, filter_weight):
    orders, rows, _, chans = grad_fourier.shape
    deg = filter_weight.shape[0]
    dq = -(-deg // 8) * 8
    width = chans // ma
    chunks = 2 * orders
    blocks = n // GROUP
    flat_rows = grad_fourier.transpose(0, 2, 1, 3).reshape(chunks, rows, chans)
    spec = jnp.pad(spectra, ((0, dq - deg), (0, 0), (0, 0), (0, 0))).transpose(1, 2, 0, 3)
    spec = spec.reshape(ma, chunks * dq, width)
    vmem = pl.BlockSpec(memory_space=pltpu.VMEM)
    dma = pltpu.SemaphoreType.DMA
    grads, wgrad = pl.pallas_call(
        functools.partial(kernel, (n, ma, orders, rows, deg, dq, chans)),
        out_shape=(
            jax.ShapeDtypeStruct((orders, 2, dq, chans), jnp.float32),
            jax.ShapeDtypeStruct((2, dq, width), jnp.float32),
        ),
        in_specs=[vmem] * 3,
        out_specs=(vmem, vmem),
        scratch_shapes=[
            pltpu.VMEM((GROUP, blocks * dq, orders * rows), jnp.bfloat16),
            pltpu.VMEM((GROUP, blocks * dq, orders * rows), jnp.bfloat16),
            pltpu.VMEM((orders, blocks * dq, GROUP * rows), jnp.bfloat16),
            pltpu.VMEM((chunks, GROUP, rows, chans), jnp.bfloat16),
            pltpu.VMEM((chunks, blocks, dq, chans), jnp.float32),
            pltpu.VMEM((chunks, blocks, dq, chans), jnp.float32),
            pltpu.VMEM((ma, chunks * dq, width), jnp.bfloat16),
            pltpu.VMEM((ma, 2, dq, width), jnp.float32),
            pltpu.VMEM((ma, 2, dq, width), jnp.float32),
            dma((GROUP,)), dma((GROUP,)),
            dma((chunks, GROUP)), dma((chunks, GROUP)),
            dma((chunks, blocks)), dma((chunks, blocks)),
            dma((ma,)), dma((ma,)),
            dma((ma,)), dma((ma,)),
        ],
        compiler_params=pltpu.CompilerParams(
            collective_id=0, has_side_effects=True, vmem_limit_bytes=24 * 1024 * 1024),
        cost_estimate=pl.CostEstimate(
            flops=2 * chunks * blocks * dq * GROUP * rows * chans, bytes_accessed=4 * chunks * dq * chans, transcendentals=0),
    )(legendre, flat_rows, spec)
    grads = grads[:, :, :deg].transpose(2, 0, 1, 3)
    real_grad = grads[:, :, 0, :]
    imag_grad = grads[:, :, 1, :]
    real_weight = filter_weight[:, None, 0, :]
    imag_weight = filter_weight[:, None, 1, :]
    input_grad = jnp.stack(
        [
            real_weight * real_grad + imag_weight * imag_grad,
            real_weight * imag_grad - imag_weight * real_grad,
        ],
        axis=2,
    )
    return input_grad, wgrad[:, :deg].transpose(1, 0, 2)


def solution(mesh):
    in_specs = (
        P("ma", "lat", None, None),
        P("ma", "lat", None),
        P("lat", None, None, "ma"),
        P("lat", None, None),
    )
    out_specs = (P("lat", "ma", None, None), P("lat", None, "ma"))
    fn = functools.partial(body, mesh.shape["lat"], mesh.shape["ma"])
    return jax.shard_map(fn, mesh=mesh, in_specs=in_specs, out_specs=out_specs, check_vma=False)
```

time: 106 us -> 39 us (0.37)
  waiting for transfers between devices: 77 us -> 0 us
  Pallas kernels: 0 us -> 34.6 us
  between operations: 14.1 us -> 0.7 us
  starting transfers between devices: 4.27 us -> 0 us
  matrix products: 3.61 us -> 0 us
  local copies, waits for them, and re-layouts: 5.9 us -> 3.51 us
    reduce_scatter x1 -> x0, waiting for transfers between devices: 63 us -> none  [body(): lax.psum_scatter(partial_value, 'lat', scatter_dimension=0, tiled=True)]
    pallas_call x0 -> x1, Pallas kernels: none -> 34.6 us  [body(): pl.pallas_call(functools.partial(kernel, (n, ma, orders, rows, deg, dq, c...]
    unnamed x3 -> x0, waiting for transfers between devices: 9.31 us -> none
    all_to_all x1 -> x0, waiting for transfers between devices: 4.68 us -> none  [body(): lax.all_to_all(spectra, 'ma', split_axis=1, concat_axis=3, tiled=True)]
    all_to_all x1 -> x0, starting transfers between devices: 4.23 us -> none  [body(): lax.all_to_all(spectra, 'ma', split_axis=1, concat_axis=3, tiled=True)]
    dot_general x1 -> x0, matrix products: 3.61 us -> none  [body(): jnp.einsum('mal,marc->lmrc', table, grad_fourier, preferred_element_type=...]
    unnamed x12 -> x8, local copies, waits for them, and re-layouts: 5.38 us -> 2.39 us
  transfers between devices with their start and end apart: 3 -> 0, of which waited for: 3 -> 0; matrix products, arithmetic and copies ran while one was open for 2% -> 0% of each run, Pallas kernels for 0% -> 0%
where the time goes in v1:
time: 39 us; the launch traced here: 38.9 us
  Pallas kernels  34.6 us (89%)
  local copies, waits for them, and re-layouts  3.51 us (9%)
  between operations  0.7 us (2%)
    pallas_call x1, Pallas kernels, body(): pl.pallas_call(functools.partial(kernel, (n, ma, orders, rows, deg, dq, c...  34.6 us
    unnamed x8, local copies, waits for them, and re-layouts  2.39 us
    transpose x1, local copies, waits for them, and re-layouts, body(): flat_rows = grad_fourier.transpose(0, 2, 1, 3).reshape(chunks, rows, chans)  0.99 us

profile of v1, /device:TPU:0, one launch (start us, length us, event | category | flops | bytes accessed | tf_op | source)
XLA Modules:
  0.0 38.9 jit_solution(7482874317960098203)
XLA Ops:
  0.6 0.0 copy-start.1
  0.6 1.0 %copy.11 = bf16[2,2,64,384]{3,2,1,0:T(8,128)(2,1)S(1)} copy(bf16[2,2,64,384]{3,1,2,0:T(2,128)(2,1)} %bitcast.14) | data formatting | bytes 393216 | tf_op jit(solution)/shard_map/transpose | solution.py:200
  1.6 0.0 copy-done.1
  1.6 0.0 copy-start
  1.7 0.9 %copy-done = bf16[2,64,640]{2,1,0:T(8,128)(2,1)S(1)} copy-done((bf16[2,64,640]{2,1,0:T(8,128)(2,1)S(1)}, bf16[2,64,640]{2,1,0:T(8,128)(2,1)}, u32[]{:S(2)}) %copy-start) | copy-done | bytes 163864
  2.6 0.0 copy-start.2
  2.6 34.6 %shard_map.59 = (f32[2,2,40,384]{3,2,1,0:T(8,128)S(1)}, f32[2,40,192]{2,1,0:T(8,128)S(1)}) custom-call(bf16[2,64,640]{2,1,0:T(8,128)(2,1)S(1)} %copy-done, bf16[4,64,384]{2,1,0:T(8,128)(2,1)S(1)} %bitcast.10, bf16[2,160,192]{2,1,0:T(8,128)(2,1)S(1)} %bitcast.11), custom_call_target="tpu_custom_call" | custom-call | flops 125829120 | bytes 245760 | tf_op jit(solution)/shard_map/pallas_call | solution.py:205
  37.2 0.0 copy-done.2
  37.2 0.1 fusion
  37.4 0.8 %copy.14 = f32[40,2,2,384]{3,2,1,0:T(2,128)} copy(f32[40,2,2,384]{3,0,2,1:T(8,128)S(1)} %pad_maximum_fusion) | data formatting | bytes 491520
  38.2 0.7 %copy.15 = f32[40,2,192]{2,1,0:T(2,128)} copy(f32[40,2,192]{2,0,1:T(8,128)S(1)} %bitcast.13) | data formatting | bytes 122880
  (4 shorter events, 0.1 us)
Async XLA Ops:
  0.6 1.0 %copy-start.1 = (bf16[40,4,2,192]{3,2,1,0:T(2,128)(2,1)S(1)}, bf16[40,4,2,192]{3,2,1,0:T(2,128)(2,1)}, u32[]{:S(2)}) copy-start(bf16[40,4,2,192]{3,2,1,0:T(2,128)(2,1)} %param.6) | copy-start | bytes 368644
  1.6 0.9 %copy-start = (bf16[2,64,640]{2,1,0:T(8,128)(2,1)S(1)}, bf16[2,64,640]{2,1,0:T(8,128)(2,1)}, u32[]{:S(2)}) copy-start(bf16[2,64,640]{2,1,0:T(8,128)(2,1)} %leg_ref.1) | copy-start | bytes 491524
  2.6 34.6 %copy-start.2 = (f32[40,2,384]{2,1,0:T(2,128)S(1)}, f32[40,2,384]{2,1,0:T(2,128)}, u32[]{:S(2)}) copy-start(f32[40,2,384]{2,1,0:T(2,128)} %param.7) | copy-start | bytes 368644

commit v2 on v1

v2 whole, which is shorter than its diff:
```python
import functools

import jax
import jax.numpy as jnp
from jax import lax
from jax.experimental import pallas as pl
from jax.experimental.pallas import tpu as pltpu
from jax.sharding import PartitionSpec as P

MESH = pl.DeviceIdType.MESH
GROUP = 8
CORE, NEAR, FAR = 1, 2, 4


def kernel(sizes, leg_hbm, rows_ref, spec_ref, grads_ref, wgrad_ref, leg_ref, tab_send, tab_all, lhs, rows_all, part,
           part_recv, value_all, spec_all, wpart, wrecv, leg_sem, tab_ssem, tab_rsem, row_ssem, row_rsem, part_ssem,
           part_rsem, spec_ssem, spec_rsem, w_ssem, w_rsem):
    n, ma, orders, rows, deg, dq, chans = sizes
    blocks = n // GROUP
    chunks = ma * orders
    width = chans // ma
    lat = lax.axis_index("lat")
    mine = lax.axis_index("ma")
    spot = lax.rem(lat, GROUP)
    block = lax.div(lat, GROUP)
    bits = [lax.rem(lax.div(spot, 1 << b), 2) for b in range(3)]

    def member(slot):
        at = 0
        for b in range(3):
            bit = 1 - bits[b] if slot >> b & 1 else bits[b]
            at = at + bit * (1 << b)
        return at

    def peer(slot):
        return (block * GROUP + member(slot), mine)

    def other_block(step):
        return lax.rem(block + step, blocks)

    def other_ma(step):
        return lax.rem(mine + step, ma)

    barrier = pltpu.get_barrier_semaphore()
    partners = [peer(slot) for slot in range(1, GROUP)]
    partners += [(other_block(step) * GROUP + spot, mine) for step in range(1, blocks)]
    partners += [(lat, other_ma(step)) for step in range(1, ma)]
    for device in partners:
        pl.semaphore_signal(barrier, inc=1, device_id=device, device_id_type=MESH)
    leg_copy = pltpu.make_async_copy(leg_hbm, leg_ref, leg_sem)
    leg_copy.start()

    for q in range(ma):
        place = lax.rem(q - mine - 1 + 2 * ma, ma)
        for m in range(orders):
            cut = slice(q * width, (q + 1) * width)
            rows_all[place * orders + m, 0] = jnp.concatenate(
                [rows_ref[2 * m][:, cut], rows_ref[2 * m + 1][:, cut]], axis=1)
    pl.semaphore_wait(barrier, len(partners))

    def copy(src, dst, ssem, rsem, device):
        return pltpu.make_async_remote_copy(
            src_ref=src, dst_ref=dst, send_sem=ssem, recv_sem=rsem, device_id=device, device_id_type=MESH)

    row_copies = {}

    def send_rows(k, have, via):
        slot = have + via
        row_copies[k, slot] = copy(rows_all.at[k, have], rows_all.at[k, slot], row_ssem.at[k, slot], row_rsem.at[k, slot],
                                   peer(via))
        row_copies[k, slot].start()

    def first(k):
        for via in (FAR, NEAR, CORE):
            send_rows(k, 0, via)

    first(0)

    leg_copy.wait()
    total = leg_ref.shape[2]
    degree = lax.broadcasted_iota(jnp.int32, (orders, rows, total), 2)
    order = lax.broadcasted_iota(jnp.int32, (orders, rows, total), 0) + mine * orders
    table = jnp.where(degree >= order, leg_ref[...].astype(jnp.float32), 0.0)
    turned = table.reshape(orders * rows, total).T
    for at in range(GROUP):
        parts = []
        for b in range(blocks):
            start = (b * GROUP + at) * deg
            part_rows = turned[start:start + deg]
            if dq > deg:
                part_rows = jnp.concatenate([part_rows, jnp.zeros((dq - deg, orders * rows), jnp.float32)], axis=0)
            parts.append(part_rows)
        tab_send[at] = jnp.concatenate(parts, axis=0).astype(jnp.bfloat16)

    tab_copies = {}
    for slot in (FAR, NEAR, FAR + NEAR, FAR + CORE, NEAR + CORE, FAR + NEAR + CORE, CORE):
        tab_copies[slot] = copy(tab_send.at[member(slot)], tab_all.at[slot], tab_ssem.at[slot], tab_rsem.at[slot], peer(slot))
        tab_copies[slot].start()
    spec_copies = []
    for step in range(1, ma):
        to = other_ma(step)
        spec_copies.append(copy(spec_ref.at[to], spec_all.at[mine], spec_ssem.at[step], spec_rsem.at[step], (lat, to)))
        spec_copies[-1].start()
    spec_all[mine] = spec_ref[mine]

    def spread(k):
        row_copies[k, FAR].wait_recv()
        send_rows(k, FAR, NEAR)
        send_rows(k, FAR, CORE)
        if k + 1 < chunks:
            first(k + 1)
        row_copies[k, NEAR].wait_recv()
        send_rows(k, NEAR, CORE)

    def spread_last(k):
        row_copies[k, FAR + NEAR].wait_recv()
        send_rows(k, FAR + NEAR, CORE)

    part_copies = {}

    def multiply(k):
        m = k % orders
        if k == 0:
            for slot in tab_copies:
                tab_copies[slot].wait_recv()
            tabs = [tab_send[spot]] + [tab_all[slot] for slot in range(1, GROUP)]
            for order_at in range(orders):
                lhs[order_at] = jnp.concatenate(
                    [t.astype(jnp.float32)[:, order_at * rows:(order_at + 1) * rows] for t in tabs], axis=1
                ).astype(jnp.bfloat16)
        for slot in (CORE, NEAR + CORE, FAR + CORE, FAR + NEAR + CORE):
            row_copies[k, slot].wait_recv()
        product = jnp.dot(lhs[m], rows_all[k].reshape(GROUP * rows, 2 * width), preferred_element_type=jnp.float32)
        part[k] = product.reshape(blocks, dq, 2 * width)
        for step in range(1, blocks):
            to = other_block(step)
            part_copies[k, step] = copy(part.at[k, to], part_recv.at[k, step], part_ssem.at[k, step], part_rsem.at[k, step],
                                        (to * GROUP + spot, mine))
            part_copies[k, step].start()

    w_copies = []

    def finish(k):
        value = part[k, block]
        for step in range(1, blocks):
            part_copies[k, step].wait_recv()
            value = value + part_recv[k, step]
        step = (k // orders + 1) % ma
        m = k % orders
        q = other_ma(step)
        value_all[q * orders + m] = value
        if k == 0:
            for each in spec_copies:
                each.wait_recv()
        real_grad = value[:, :width]
        imag_grad = value[:, width:]
        stored = spec_all[q].astype(jnp.float32)
        real_store = stored[2 * m * dq:(2 * m + 1) * dq]
        imag_store = stored[(2 * m + 1) * dq:(2 * m + 2) * dq]
        real = real_store * real_grad + imag_store * imag_grad
        imag = real_store * imag_grad - imag_store * real_grad
        if m == 0:
            wpart[step, 0] = real
            wpart[step, 1] = imag
        else:
            wpart[step, 0] += real
            wpart[step, 1] += imag
        if m == orders - 1 and step > 0:
            w_copies.append(copy(wpart.at[step], wrecv.at[step], w_ssem.at[step], w_rsem.at[step], (lat, q)))
            w_copies[-1].start()

    spread(0)
    spread_last(0)
    for k in range(chunks):
        if k + 1 < chunks:
            spread(k + 1)
        multiply(k)
        if k + 1 < chunks:
            spread_last(k + 1)
        if k >= 1:
            finish(k - 1)
    finish(chunks - 1)

    for m in range(orders):
        for r in range(2):
            grads_ref[m, r] = jnp.concatenate(
                [value_all[q * orders + m][:, r * width:(r + 1) * width] for q in range(ma)], axis=1)
    weight = wpart[0]
    for step in range(1, ma):
        w_copies[step - 1].wait_recv()
        weight = weight + wrecv[step]
    wgrad_ref[...] = weight

    for each in [*tab_copies.values(), *row_copies.values(), *part_copies.values(), *spec_copies, *w_copies]:
        each.wait_send()


def body(n, ma, grad_fourier, legendre, spectra, filter_weight):
    orders, rows, _, chans = grad_fourier.shape
    deg = filter_weight.shape[0]
    dq = -(-deg // 8) * 8
    width = chans // ma
    chunks = ma * orders
    blocks = n // GROUP
    flat_rows = grad_fourier.transpose(0, 2, 1, 3).reshape(2 * orders, rows, chans)
    spec = jnp.pad(spectra, ((0, dq - deg), (0, 0), (0, 0), (0, 0))).transpose(1, 2, 0, 3)
    spec = spec.reshape(ma, 2 * orders * dq, width)
    vmem = pl.BlockSpec(memory_space=pltpu.VMEM)
    dma = pltpu.SemaphoreType.DMA
    grads, wgrad = pl.pallas_call(
        functools.partial(kernel, (n, ma, orders, rows, deg, dq, chans)),
        out_shape=(
            jax.ShapeDtypeStruct((orders, 2, dq, chans), jnp.float32),
            jax.ShapeDtypeStruct((2, dq, width), jnp.float32),
        ),
        in_specs=[pl.BlockSpec(memory_space=pltpu.HBM), vmem, vmem],
        out_specs=(vmem, vmem),
        scratch_shapes=[
            pltpu.VMEM(legendre.shape, jnp.bfloat16),
            pltpu.VMEM((GROUP, blocks * dq, orders * rows), jnp.bfloat16),
            pltpu.VMEM((GROUP, blocks * dq, orders * rows), jnp.bfloat16),
            pltpu.VMEM((orders, blocks * dq, GROUP * rows), jnp.bfloat16),
            pltpu.VMEM((chunks, GROUP, rows, 2 * width), jnp.bfloat16),
            pltpu.VMEM((chunks, blocks, dq, 2 * width), jnp.float32),
            pltpu.VMEM((chunks, blocks, dq, 2 * width), jnp.float32),
            pltpu.VMEM((chunks, dq, 2 * width), jnp.float32),
            pltpu.VMEM((ma, 2 * orders * dq, width), jnp.bfloat16),
            pltpu.VMEM((ma, 2, dq, width), jnp.float32),
            pltpu.VMEM((ma, 2, dq, width), jnp.float32),
            dma(()),
            dma((GROUP,)), dma((GROUP,)),
            dma((chunks, GROUP)), dma((chunks, GROUP)),
            dma((chunks, blocks)), dma((chunks, blocks)),
            dma((ma,)), dma((ma,)),
            dma((ma,)), dma((ma,)),
        ],
        compiler_params=pltpu.CompilerParams(
            collective_id=0, has_side_effects=True, vmem_limit_bytes=24 * 1024 * 1024),
        cost_estimate=pl.CostEstimate(
            flops=4 * orders * blocks * dq * GROUP * rows * chans, bytes_accessed=8 * orders * dq * chans, transcendentals=0),
    )(legendre, flat_rows, spec)
    grads = grads[:, :, :deg].transpose(2, 0, 1, 3)
    real_grad = grads[:, :, 0, :]
    imag_grad = grads[:, :, 1, :]
    real_weight = filter_weight[:, None, 0, :]
    imag_weight = filter_weight[:, None, 1, :]
    input_grad = jnp.stack(
        [
            real_weight * real_grad + imag_weight * imag_grad,
            real_weight * imag_grad - imag_weight * real_grad,
        ],
        axis=2,
    )
    return input_grad, wgrad[:, :deg].transpose(1, 0, 2)


def solution(mesh):
    in_specs = (
        P("ma", "lat", None, None),
        P("ma", "lat", None),
        P("lat", None, None, "ma"),
        P("lat", None, None),
    )
    out_specs = (P("lat", "ma", None, None), P("lat", None, "ma"))
    fn = functools.partial(body, mesh.shape["lat"], mesh.shape["ma"])
    return jax.shard_map(fn, mesh=mesh, in_specs=in_specs, out_specs=out_specs, check_vma=False)
```

time: 39 us -> 33.3 us (0.85)
  Pallas kernels: 34.6 us -> 28.9 us
    pallas_call x1, Pallas kernels: 34.6 us -> 28.9 us  [body(): pl.pallas_call(functools.partial(kernel, (n, ma, orders, rows, deg, dq, c...]
where the time goes in v2:
time: 33.3 us; the launch traced here: 33.1 us
  Pallas kernels  28.9 us (87%)
  local copies, waits for them, and re-layouts  3.51 us (11%)
  between operations  0.7 us (2%)
    pallas_call x1, Pallas kernels, body(): pl.pallas_call(functools.partial(kernel, (n, ma, orders, rows, deg, dq, c...  28.9 us
    unnamed x8, local copies, waits for them, and re-layouts  2.39 us
    transpose x1, local copies, waits for them, and re-layouts, body(): grad_fourier.transpose(0, 2, 1, 3).reshape(2 * orders, rows, chans)  0.99 us

profile of v2, /device:TPU:0, one launch (start us, length us, event | category | flops | bytes accessed | tf_op | source)
XLA Modules:
  0.0 33.1 jit_solution(9690215101770613357)
XLA Ops:
  0.6 0.0 copy-start.1
  0.6 1.0 %copy.11 = bf16[2,2,64,384]{3,2,1,0:T(8,128)(2,1)S(1)} copy(bf16[2,2,64,384]{3,1,2,0:T(2,128)(2,1)} %bitcast.14) | data formatting | bytes 393216 | tf_op jit(solution)/shard_map/transpose | solution.py:205
  1.6 0.0 copy-done.1
  1.6 0.0 copy-start
  1.7 0.9 %copy-done = bf16[2,64,640]{2,1,0:T(8,128)(2,1)S(1)} copy-done((bf16[2,64,640]{2,1,0:T(8,128)(2,1)S(1)}, bf16[2,64,640]{2,1,0:T(8,128)(2,1)}, u32[]{:S(2)}) %copy-start) | copy-done | bytes 163864
  2.6 0.0 copy-start.2
  2.6 28.9 %shard_map.59 = (f32[2,2,40,384]{3,2,1,0:T(8,128)S(1)}, f32[2,40,192]{2,1,0:T(8,128)S(1)}) custom-call(bf16[2,64,640]{2,1,0:T(8,128)(2,1)S(1)} %copy-done, bf16[4,64,384]{2,1,0:T(8,128)(2,1)S(1)} %bitcast.10, bf16[2,160,192]{2,1,0:T(8,128)(2,1)S(1)} %bitcast.11), custom_call_target="tpu_custom_call" | custom-call | flops 125829120 | bytes 245760 | tf_op jit(solution)/shard_map/pallas_call | solution.py:210
  31.5 0.0 copy-done.2
  31.5 0.1 fusion
  31.7 0.8 %copy.14 = f32[40,2,2,384]{3,2,1,0:T(2,128)} copy(f32[40,2,2,384]{3,0,2,1:T(8,128)S(1)} %pad_maximum_fusion) | data formatting | bytes 491520
  32.5 0.7 %copy.15 = f32[40,2,192]{2,1,0:T(2,128)} copy(f32[40,2,192]{2,0,1:T(8,128)S(1)} %bitcast.13) | data formatting | bytes 122880
  (4 shorter events, 0.1 us)
Async XLA Ops:
  0.6 1.0 %copy-start.1 = (bf16[40,4,2,192]{3,2,1,0:T(2,128)(2,1)S(1)}, bf16[40,4,2,192]{3,2,1,0:T(2,128)(2,1)}, u32[]{:S(2)}) copy-start(bf16[40,4,2,192]{3,2,1,0:T(2,128)(2,1)} %param.6) | copy-start | bytes 368644
  1.6 0.9 %copy-start = (bf16[2,64,640]{2,1,0:T(8,128)(2,1)S(1)}, bf16[2,64,640]{2,1,0:T(8,128)(2,1)}, u32[]{:S(2)}) copy-start(bf16[2,64,640]{2,1,0:T(8,128)(2,1)} %leg_hbm.1) | copy-start | bytes 491524
  2.6 28.9 %copy-start.2 = (f32[40,2,384]{2,1,0:T(2,128)S(1)}, f32[40,2,384]{2,1,0:T(2,128)}, u32[]{:S(2)}) copy-start(f32[40,2,384]{2,1,0:T(2,128)} %param.7) | copy-start | bytes 368644

commit v3 on v2

--- a/solution.py
+++ b/solution.py
@@ -177,9 +177,8 @@
         multiply(k)
         if k + 1 < chunks:
             spread_last(k + 1)
-        if k >= 1:
-            finish(k - 1)
-    finish(chunks - 1)
+    for k in range(chunks):
+        finish(k)
 
     for m in range(orders):
         for r in range(2):

time: 33.3 us -> 32.8 us (0.985)
  Pallas kernels: 28.9 us -> 28.3 us
    pallas_call x1, Pallas kernels: 28.9 us -> 28.3 us  [body(): pl.pallas_call(functools.partial(kernel, (n, ma, orders, rows, deg, dq, c...]
where the time goes in v3:
time: 32.8 us; the launch traced here: 32.6 us
  Pallas kernels  28.3 us (86%)
  local copies, waits for them, and re-layouts  3.51 us (11%)
  between operations  0.7 us (2%)
    pallas_call x1, Pallas kernels, body(): pl.pallas_call(functools.partial(kernel, (n, ma, orders, rows, deg, dq, c...  28.3 us
    unnamed x8, local copies, waits for them, and re-layouts  2.39 us
    transpose x1, local copies, waits for them, and re-layouts, body(): grad_fourier.transpose(0, 2, 1, 3).reshape(2 * orders, rows, chans)  0.99 us

profile of v3, /device:TPU:0, one launch (start us, length us, event | category | flops | bytes accessed | tf_op | source)
XLA Modules:
  0.0 32.6 jit_solution(2155335393790252169)
XLA Ops:
  0.6 0.0 copy-start.1
  0.6 1.0 %copy.11 = bf16[2,2,64,384]{3,2,1,0:T(8,128)(2,1)S(1)} copy(bf16[2,2,64,384]{3,1,2,0:T(2,128)(2,1)} %bitcast.14) | data formatting | bytes 393216 | tf_op jit(solution)/shard_map/transpose | solution.py:204
  1.6 0.0 copy-done.1
  1.6 0.0 copy-start
  1.7 0.9 %copy-done = bf16[2,64,640]{2,1,0:T(8,128)(2,1)S(1)} copy-done((bf16[2,64,640]{2,1,0:T(8,128)(2,1)S(1)}, bf16[2,64,640]{2,1,0:T(8,128)(2,1)}, u32[]{:S(2)}) %copy-start) | copy-done | bytes 163864
  2.6 0.0 copy-start.2
  2.6 28.3 %shard_map.59 = (f32[2,2,40,384]{3,2,1,0:T(8,128)S(1)}, f32[2,40,192]{2,1,0:T(8,128)S(1)}) custom-call(bf16[2,64,640]{2,1,0:T(8,128)(2,1)S(1)} %copy-done, bf16[4,64,384]{2,1,0:T(8,128)(2,1)S(1)} %bitcast.10, bf16[2,160,192]{2,1,0:T(8,128)(2,1)S(1)} %bitcast.11), custom_call_target="tpu_custom_call" | custom-call | flops 125829120 | bytes 245760 | tf_op jit(solution)/shard_map/pallas_call | solution.py:209
  30.9 0.0 copy-done.2
  30.9 0.1 fusion
  31.1 0.8 %copy.14 = f32[40,2,2,384]{3,2,1,0:T(2,128)} copy(f32[40,2,2,384]{3,0,2,1:T(8,128)S(1)} %pad_maximum_fusion) | data formatting | bytes 491520
  31.9 0.7 %copy.15 = f32[40,2,192]{2,1,0:T(2,128)} copy(f32[40,2,192]{2,0,1:T(8,128)S(1)} %bitcast.13) | data formatting | bytes 122880
  (4 shorter events, 0.1 us)
Async XLA Ops:
  0.6 1.0 %copy-start.1 = (bf16[40,4,2,192]{3,2,1,0:T(2,128)(2,1)S(1)}, bf16[40,4,2,192]{3,2,1,0:T(2,128)(2,1)}, u32[]{:S(2)}) copy-start(bf16[40,4,2,192]{3,2,1,0:T(2,128)(2,1)} %param.6) | copy-start | bytes 368644
  1.6 0.9 %copy-start = (bf16[2,64,640]{2,1,0:T(8,128)(2,1)S(1)}, bf16[2,64,640]{2,1,0:T(8,128)(2,1)}, u32[]{:S(2)}) copy-start(bf16[2,64,640]{2,1,0:T(8,128)(2,1)} %leg_hbm.1) | copy-start | bytes 491524
  2.6 28.3 %copy-start.2 = (f32[40,2,384]{2,1,0:T(2,128)S(1)}, f32[40,2,384]{2,1,0:T(2,128)}, u32[]{:S(2)}) copy-start(f32[40,2,384]{2,1,0:T(2,128)} %param.7) | copy-start | bytes 368644

commit v4 on v3

--- a/solution.py
+++ b/solution.py
@@ -12,9 +12,9 @@
 CORE, NEAR, FAR = 1, 2, 4
 
 
-def kernel(sizes, leg_hbm, rows_ref, spec_ref, grads_ref, wgrad_ref, leg_ref, tab_send, tab_all, lhs, rows_all, part,
-           part_recv, value_all, spec_all, wpart, wrecv, leg_sem, tab_ssem, tab_rsem, row_ssem, row_rsem, part_ssem,
-           part_rsem, spec_ssem, spec_rsem, w_ssem, w_rsem):
+def kernel(sizes, grad_hbm, leg_hbm, spec_hbm, filter_hbm, input_ref, wgrad_ref, grad_ref, leg_ref, raw_ref, filter_ref,
+           tab_send, tab_all, lhs, rows_all, part, part_recv, value_all, spec_send, spec_all, wpart, wrecv, in_sem, tab_ssem,
+           tab_rsem, row_ssem, row_rsem, part_ssem, part_rsem, spec_ssem, spec_rsem, w_ssem, w_rsem):
     n, ma, orders, rows, deg, dq, chans = sizes
     blocks = n // GROUP
     chunks = ma * orders
@@ -47,15 +47,21 @@
     partners += [(lat, other_ma(step)) for step in range(1, ma)]
     for device in partners:
         pl.semaphore_signal(barrier, inc=1, device_id=device, device_id_type=MESH)
-    leg_copy = pltpu.make_async_copy(leg_hbm, leg_ref, leg_sem)
-    leg_copy.start()
-
-    for q in range(ma):
-        place = lax.rem(q - mine - 1 + 2 * ma, ma)
-        for m in range(orders):
+    loads = []
+    for at, (far, near) in enumerate(((grad_hbm, grad_ref), (leg_hbm, leg_ref), (spec_hbm, raw_ref), (filter_hbm, filter_ref))):
+        loads.append(pltpu.make_async_copy(far, near, in_sem.at[at]))
+        loads[-1].start()
+
+    def stage(m):
+        halves = grad_ref[m].astype(jnp.float32)
+        halves = [halves[:, r, :].astype(jnp.bfloat16) for r in range(2)]
+        for q in range(ma):
+            place = lax.rem(q - mine - 1 + 2 * ma, ma)
             cut = slice(q * width, (q + 1) * width)
-            rows_all[place * orders + m, 0] = jnp.concatenate(
-                [rows_ref[2 * m][:, cut], rows_ref[2 * m + 1][:, cut]], axis=1)
+            rows_all[place * orders + m, 0] = jnp.concatenate([half[:, cut] for half in halves], axis=1)
+
+    loads[0].wait()
+    stage(0)
     pl.semaphore_wait(barrier, len(partners))
 
     def copy(src, dst, ssem, rsem, device):
@@ -76,7 +82,7 @@
 
     first(0)
 
-    leg_copy.wait()
+    loads[1].wait()
     total = leg_ref.shape[2]
     degree = lax.broadcasted_iota(jnp.int32, (orders, rows, total), 2)
     order = lax.broadcasted_iota(jnp.int32, (orders, rows, total), 0) + mine * orders
@@ -96,12 +102,26 @@
     for slot in (FAR, NEAR, FAR + NEAR, FAR + CORE, NEAR + CORE, FAR + NEAR + CORE, CORE):
         tab_copies[slot] = copy(tab_send.at[member(slot)], tab_all.at[slot], tab_ssem.at[slot], tab_rsem.at[slot], peer(slot))
         tab_copies[slot].start()
+    for m in range(1, orders):
+        stage(m)
     spec_copies = []
-    for step in range(1, ma):
-        to = other_ma(step)
-        spec_copies.append(copy(spec_ref.at[to], spec_all.at[mine], spec_ssem.at[step], spec_rsem.at[step], (lat, to)))
-        spec_copies[-1].start()
-    spec_all[mine] = spec_ref[mine]
+
+    def send_spectra():
+        loads[2].wait()
+        raw = raw_ref[...].astype(jnp.float32)
+        for q in range(ma):
+            parts = []
+            for m in range(orders):
+                for r in range(2):
+                    parts.append(raw[:, q * orders + m, r, :])
+                    if dq > deg:
+                        parts.append(jnp.zeros((dq - deg, width), jnp.float32))
+            spec_send[q] = jnp.concatenate(parts, axis=0).astype(jnp.bfloat16)
+        for step in range(1, ma):
+            to = other_ma(step)
+            spec_copies.append(copy(spec_send.at[to], spec_all.at[mine], spec_ssem.at[step], spec_rsem.at[step], (lat, to)))
+            spec_copies[-1].start()
+        spec_all[mine] = spec_send[mine]
 
     def spread(k):
         row_copies[k, FAR].wait_recv()
@@ -175,20 +195,28 @@
         if k + 1 < chunks:
             spread(k + 1)
         multiply(k)
+        if k == 0:
+            send_spectra()
         if k + 1 < chunks:
             spread_last(k + 1)
+
+    loads[3].wait()
+    real_weight, imag_weight = [filter_ref[:, r, :] for r in range(2)]
     for k in range(chunks):
         finish(k)
-
-    for m in range(orders):
-        for r in range(2):
-            grads_ref[m, r] = jnp.concatenate(
-                [value_all[q * orders + m][:, r * width:(r + 1) * width] for q in range(ma)], axis=1)
+        if k >= chunks - orders:
+            m = k % orders
+            real_grad, imag_grad = [
+                jnp.concatenate([value_all[q * orders + m][:deg, r * width:(r + 1) * width] for q in range(ma)], axis=1)
+                for r in range(2)]
+            input_ref[:, m, 0, :] = real_weight * real_grad + imag_weight * imag_grad
+            input_ref[:, m, 1, :] = real_weight * imag_grad - imag_weight * real_grad
     weight = wpart[0]
     for step in range(1, ma):
         w_copies[step - 1].wait_recv()
         weight = weight + wrecv[step]
-    wgrad_ref[...] = weight
+    for r in range(2):
+        wgrad_ref[:, r, :] = weight[r, :deg]
 
     for each in [*tab_copies.values(), *row_copies.values(), *part_copies.values(), *spec_copies, *w_copies]:
         each.wait_send()
@@ -201,21 +229,21 @@
     width = chans // ma
     chunks = ma * orders
     blocks = n // GROUP
-    flat_rows = grad_fourier.transpose(0, 2, 1, 3).reshape(2 * orders, rows, chans)
-    spec = jnp.pad(spectra, ((0, dq - deg), (0, 0), (0, 0), (0, 0))).transpose(1, 2, 0, 3)
-    spec = spec.reshape(ma, 2 * orders * dq, width)
     vmem = pl.BlockSpec(memory_space=pltpu.VMEM)
     dma = pltpu.SemaphoreType.DMA
-    grads, wgrad = pl.pallas_call(
+    return pl.pallas_call(
         functools.partial(kernel, (n, ma, orders, rows, deg, dq, chans)),
         out_shape=(
-            jax.ShapeDtypeStruct((orders, 2, dq, chans), jnp.float32),
-            jax.ShapeDtypeStruct((2, dq, width), jnp.float32),
+            jax.ShapeDtypeStruct((deg, orders, 2, chans), jnp.float32),
+            jax.ShapeDtypeStruct((deg, 2, width), jnp.float32),
         ),
-        in_specs=[pl.BlockSpec(memory_space=pltpu.HBM), vmem, vmem],
+        in_specs=[pl.BlockSpec(memory_space=pltpu.HBM)] * 4,
         out_specs=(vmem, vmem),
         scratch_shapes=[
+            pltpu.VMEM(grad_fourier.shape, jnp.bfloat16),
             pltpu.VMEM(legendre.shape, jnp.bfloat16),
+            pltpu.VMEM(spectra.shape, jnp.bfloat16),
+            pltpu.VMEM(filter_weight.shape, jnp.float32),
             pltpu.VMEM((GROUP, blocks * dq, orders * rows), jnp.bfloat16),
             pltpu.VMEM((GROUP, blocks * dq, orders * rows), jnp.bfloat16),
             pltpu.VMEM((orders, blocks * dq, GROUP * rows), jnp.bfloat16),
@@ -224,9 +252,10 @@
             pltpu.VMEM((chunks, blocks, dq, 2 * width), jnp.float32),
             pltpu.VMEM((chunks, dq, 2 * width), jnp.float32),
             pltpu.VMEM((ma, 2 * orders * dq, width), jnp.bfloat16),
+            pltpu.VMEM((ma, 2 * orders * dq, width), jnp.bfloat16),
             pltpu.VMEM((ma, 2, dq, width), jnp.float32),
             pltpu.VMEM((ma, 2, dq, width), jnp.float32),
-            dma(()),
+            dma((4,)),
             dma((GROUP,)), dma((GROUP,)),
             dma((chunks, GROUP)), dma((chunks, GROUP)),
             dma((chunks, blocks)), dma((chunks, blocks)),
@@ -234,23 +263,10 @@
             dma((ma,)), dma((ma,)),
         ],
         compiler_params=pltpu.CompilerParams(
-            collective_id=0, has_side_effects=True, vmem_limit_bytes=24 * 1024 * 1024),
+            collective_id=0, has_side_effects=True, vmem_limit_bytes=60 * 1024 * 1024),
         cost_estimate=pl.CostEstimate(
             flops=4 * orders * blocks * dq * GROUP * rows * chans, bytes_accessed=8 * orders * dq * chans, transcendentals=0),
-    )(legendre, flat_rows, spec)
-    grads = grads[:, :, :deg].transpose(2, 0, 1, 3)
-    real_grad = grads[:, :, 0, :]
-    imag_grad = grads[:, :, 1, :]
-    real_weight = filter_weight[:, None, 0, :]
-    imag_weight = filter_weight[:, None, 1, :]
-    input_grad = jnp.stack(
-        [
-            real_weight * real_grad + imag_weight * imag_grad,
-            real_weight * imag_grad - imag_weight * real_grad,
-        ],
-        axis=2,
-    )
-    return input_grad, wgrad[:, :deg].transpose(1, 0, 2)
+    )(grad_fourier, legendre, spectra, filter_weight)
 
 
 def solution(mesh):

time: 32.8 us -> 32.4 us (0.988)
  local copies, waits for them, and re-layouts: 3.51 us -> 2.37 us
  Pallas kernels: 28.3 us -> 29.2 us
    transpose x2 -> x0, local copies, waits for them, and re-layouts: 1.02 us -> none  [the longest x1 0.99 us: body(): grad_fourier.transpose(0, 2, 1, 3).reshape(2 * orders, rows, chans)]
    pallas_call x1, Pallas kernels: 28.3 us -> 29.2 us  [body(): pl.pallas_call(functools.partial(kernel, (n, ma, orders, rows, deg, dq, c...]
    unnamed x8 -> x4, local copies, waits for them, and re-layouts: 2.39 us -> 2.37 us
where the time goes in v4:
time: 32.4 us; the launch traced here: 32.2 us
  Pallas kernels  29.2 us (90%)
  local copies, waits for them, and re-layouts  2.37 us (7%)
  between operations  0.65 us (2%)
    pallas_call x1, Pallas kernels, body(): pl.pallas_call(functools.partial(kernel, (n, ma, orders, rows, deg, dq, c...  29.2 us
    unnamed x4, local copies, waits for them, and re-layouts  2.37 us

profile of v4, /device:TPU:0, one launch (start us, length us, event | category | flops | bytes accessed | tf_op | source)
XLA Modules:
  0.0 32.2 jit_solution(11540943480905633106)
XLA Ops:
  0.6 29.2 %shard_map.59 = (f32[40,2,2,384]{3,2,1,0:T(2,128)}, f32[40,2,192]{2,1,0:T(2,128)}) custom-call(bf16[2,64,2,384]{3,2,1,0:T(2,128)(2,1)} %grad_hbm.1, bf16[2,64,640]{2,1,0:T(8,128)(2,1)} %leg_hbm.1, bf16[40,4,2,192]{3,2,1,0:T(2,128)(2,1)} %spec_hbm.1, f32[40,2,384]{2,1,0:T(2,128)} %filter_hbm.1), custom_call_target="tpu_custom_call" | custom-call | flops 125829120 | bytes 245760 | tf_op jit(solution)/shard_map/pallas_call | solution.py:234
  29.8 0.0 copy-start
  29.9 1.7 %copy.8 = f32[40,2,2,384]{3,2,1,0:T(2,128)} copy(f32[40,2,2,384]{3,2,1,0:T(2,128)} %get-tuple-element.4) | data formatting | bytes 491520
  31.6 0.0 copy-done
  31.6 0.6 %copy.9 = f32[40,2,192]{2,1,0:T(2,128)} copy(f32[40,2,192]{2,1,0:T(2,128)S(1)} %copy-done) | data formatting | bytes 122880
Async XLA Ops:
  29.8 1.7 %copy-start = (f32[40,2,192]{2,1,0:T(2,128)S(1)}, f32[40,2,192]{2,1,0:T(2,128)}, u32[]{:S(2)}) copy-start(f32[40,2,192]{2,1,0:T(2,128)} %get-tuple-element.5) | copy-start | bytes 184324
